TPU v7x, 32 devices: a whole 2x2x4 slice. The times are simulated.
32 devices in a mesh: parts: 2 (over y), seq: 4 (over z), mp: 2 (over x), rep: 2 (over core).
Axes of the slice: x: 2, y: 2, z: 4, core: 2. Of those that a mesh axis runs over, the one named last changes fastest.
Arguments:
- queries: bfloat16 [6144, 4096], P(('parts', 'seq'), ('mp', 'rep')), parts along dimension 0, may hold values from -110 to 110
- key_weight: bfloat16 [1024, 4096], P(None, ('mp', 'rep')), may hold values from -0.1875 to 0.1875
- value_weight: bfloat16 [1024, 4096], P(None, ('mp', 'rep')), may hold values from -0.1875 to 0.1875
- enc_gain: float32 [1024], P(('mp', 'rep')), may hold values from 0.25 to 1.75
- store: bfloat16 [128, 128, 1024], P(('parts', 'seq'), None, ('mp', 'rep')), parts along dimension 0, may hold values from -330 to 330
- nbr_owner: int32 [96, 2], P(('parts', 'seq')), parts along dimension 0, may hold values from 0 to 3, all different within a row; in each aligned block of 12 rows (0 to 11, 12 to 23, ...) at most 12 rows name the same one
- nbr_slot: int32 [96, 2], P(('parts', 'seq')), parts along dimension 0, may hold values from 0 to 15
- nbr_count: int32 [96], P(('parts', 'seq')), parts along dimension 0, may hold values from 1 to 2
Outputs:
- attended: bfloat16 [6144, 4096], P(('parts', 'seq'), ('mp', 'rep')), parts along dimension 0
There are 2 independent parts, one for each index of `parts`. A program takes and returns all parts, laid end to end along the dimension named above; an argument that names none is the same for every part. Nothing has to cross between parts.
Inputs may be any that keep to these rules, and one draw needn't show every extreme that they name: `nbr_owner`: in each aligned block of 12 stretches no owner is named more than 12 times, and the 2 owners of one stretch differ.
All inputs are finite; a program needn't handle non-finite values.
Results may differ from a plain program's by a relative error of at most 0.0089.
Values may be sent and summed in bfloat16 or wider, within the bound.
No kernel may reach another device: no remote copies, remote signals or barrier semaphores. Data moves between devices by JAX's collectives and lax.ppermute only.
A program may use at most 128 MiB of HBM per device.

v0:
```python
import math

import jax
import jax.numpy as jnp
from jax import lax
from jax.sharding import PartitionSpec as P

HEAD_DIM = 128
DE = 1024
NLEN = 128
STRETCH = 64
KMAX = 2


EPS = 1e-06


def from_behind(value, axis, steps):
    count = lax.axis_size(axis)
    first, last = (max(0, -steps), min(count, count - steps))
    return lax.ppermute(value, axis, [(source, source + steps) for source in range(first, last)])


def attend(query_blocks, key_blocks, value_blocks, present):
    groups, width, columns = query_blocks.shape
    heads = columns // HEAD_DIM
    span = key_blocks.shape[1]
    kinds = present.shape[1]
    queried = query_blocks.reshape(groups, width, heads, HEAD_DIM)
    keyed = key_blocks.reshape(groups, span, heads, HEAD_DIM)
    valued = value_blocks.reshape(groups, span, heads, HEAD_DIM)
    scores = jnp.einsum("gqhd,gkhd->ghqk", queried, keyed, preferred_element_type=jnp.float32) * (
        1.0 / math.sqrt(HEAD_DIM)
    )
    allowed = jnp.broadcast_to(present[:, :, None], (groups, kinds, span // kinds)).reshape(
        groups, span
    )
    scores = jnp.where(allowed[:, None, None, :], scores, -1e30)
    top = jnp.max(scores, axis=3, keepdims=True)
    expo = jnp.exp(scores - top)
    weights = (expo / jnp.sum(expo, axis=3, keepdims=True)).astype(jnp.bfloat16)
    mixed = jnp.einsum("ghqk,gkhd->gqhd", weights, valued, preferred_element_type=jnp.float32)
    filled = jnp.any(present, axis=1)
    mixed = jnp.where(filled[:, None, None, None], mixed, 0.0)
    return mixed.astype(jnp.bfloat16).reshape(groups, width, columns)


def body(queries, key_weight, value_weight, enc_gain, store, nbr_owner, nbr_slot, nbr_count):
    owners_axis = lax.axis_size("seq")
    local_stretches = nbr_owner.shape[0]
    depth = max(2, 2 * local_stretches * KMAX // owners_axis)
    raw = store.astype(jnp.float32)
    squares = lax.psum(jnp.sum(raw * raw, axis=2), ("mp", "rep"))
    normed = (raw * lax.rsqrt(squares / DE + EPS)[:, :, None] * enc_gain).astype(jnp.bfloat16)
    columns = key_weight.shape[1]
    query_blocks = queries.reshape(local_stretches, STRETCH, columns)
    owners = nbr_owner.reshape(-1)
    slots = nbr_slot.reshape(-1)
    count = owners.shape[0]
    order = jnp.arange(count, dtype=jnp.int32)
    before = (owners[:, None] == owners[None, :]) & (order[None, :] < order[:, None])
    rank = jnp.sum(before.astype(jnp.int32), axis=1)
    target = owners * depth + rank
    hits = target[:, None] == jnp.arange(owners_axis * depth, dtype=jnp.int32)[None, :]
    table = jnp.sum(jnp.where(hits, slots[:, None], 0), axis=0)
    table = table.reshape(owners_axis, depth)
    arrived = lax.all_to_all(
        normed[lax.all_to_all(table, "seq", split_axis=0, concat_axis=0, tiled=True)],
        "seq",
        split_axis=0,
        concat_axis=0,
        tiled=True,
    )
    fetched = arrived.reshape(owners_axis * depth, NLEN, arrived.shape[3])[target]
    rows = count * NLEN
    piece = lax.all_gather(fetched, ("mp", "rep"), axis=2, tiled=True)
    flat = piece.reshape(rows, piece.shape[2])
    keys = jnp.dot(flat, key_weight, preferred_element_type=jnp.float32)
    values = jnp.dot(flat, value_weight, preferred_element_type=jnp.float32)
    groups = nbr_owner.shape[0]
    keys = keys.astype(jnp.bfloat16).reshape(groups, KMAX * NLEN, columns)
    values = values.astype(jnp.bfloat16).reshape(groups, KMAX * NLEN, columns)
    keys, values = (keys, values)
    present = (jnp.arange(KMAX, dtype=jnp.int32)[None, :] < nbr_count[:, None]).astype(jnp.bfloat16)
    moved_keys, moved_values, moved_present = from_behind(
        (keys[-1], values[-1], present[-1]), "seq", 1
    )
    keys = jnp.concatenate([moved_keys[None], keys[:-1]], axis=0)
    values = jnp.concatenate([moved_values[None], values[:-1]], axis=0)
    present = jnp.concatenate([moved_present[None], present[:-1]], axis=0) > 0.5
    result = attend(query_blocks, keys, values, present)
    return result.reshape(local_stretches * STRETCH, columns)


def solution(mesh):
    in_specs = (
        P(("parts", "seq"), ("mp", "rep")),
        P(None, ("mp", "rep")),
        P(None, ("mp", "rep")),
        P(("mp", "rep")),
        P(("parts", "seq"), None, ("mp", "rep")),
        P(("parts", "seq"), None),
        P(("parts", "seq"), None),
        P(("parts", "seq")),
    )
    out_specs = P(("parts", "seq"), ("mp", "rep"))
    return jax.shard_map(body, mesh=mesh, in_specs=in_specs, out_specs=out_specs, check_vma=False)
```

profile of v0, /device:TPU:0, one launch (start us, length us, event | category | flops | bytes accessed | tf_op | source)
XLA Modules:
  0.0 223.3 jit_solution(9600694696207405303)
XLA Ops:
  9.3 6.3 %all-to-all-start = ((s32[4,1,12]{2,1,0:T(1,128)}), s32[4,1,12]{2,1,0:T(1,128)S(1)}, u32[]{:S(2)}, u32[]{:S(2)}) async-start(s32[4,1,12]{2,1,0:T(1,128)} %bitcast.1), calls=%async_computation | async-start | bytes 4096 | tf_op jit(solution)/shard_map/all_to_all | solution.py:68
  15.7 1.6 fusion.17
  17.2 6.5 %psum.7 = f32[16,128]{1,0:T(8,128)S(1)} all-reduce(f32[16,128]{1,0:T(8,128)S(1)} %fusion.17), channel_id=1, replica_groups=mesh['parts'=2,'seq'=4,'mp'=2,'rep'=2] {'mp','rep'}, use_global_device_ids=true, to_apply=%region_2.0 | all-reduce | flops 2048 | bytes 16384 | tf_op jit(solution)/shard_map/psum | solution.py:53
  23.7 1.6 fusion.19
  25.4 2.6 %gather_fusion = bf16[48,128,256]{2,1,0:T(8,128)(2,1)} fusion(bf16[16,128,256]{2,1,0:T(8,128)(2,1)S(1)} %fusion.19, s32[1024]{0:T(1024)S(1)} %pad_clamp_fusion.1), kind=kCustom, calls=%fused_computation | custom fusion | bytes 6291648 | tf_op jit(solution)/shard_map/gather | solution.py:68
  28.0 4.9 %all-to-all-start.1 = ((bf16[4,12,128,256]{3,2,1,0:T(8,128)(2,1)}), bf16[4,12,128,256]{3,2,1,0:T(8,128)(2,1)}, u32[]{:S(2)}, u32[]{:S(2)}) async-start(bf16[4,12,128,256]{3,2,1,0:T(8,128)(2,1)} %bitcast.59), calls=%async_computation.1 | async-start | bytes 6291456 | tf_op jit(solution)/shard_map/all_to_all | solution.py:67
  33.1 70.3 %all-to-all-done.1 = bf16[4,12,128,256]{3,2,1,0:T(8,128)(2,1)} async-done(((bf16[4,12,128,256]{3,2,1,0:T(8,128)(2,1)}), bf16[4,12,128,256]{3,2,1,0:T(8,128)(2,1)}, u32[]{:S(2)}, u32[]{:S(2)}) %all-to-all-start.1) | async-done | bytes 3145760 | tf_op jit(solution)/shard_map/all_to_all | solution.py:67
  103.4 3.7 %gather_fusion.1 = bf16[24,128,256]{2,1,0:T(8,128)(2,1)} fusion(bf16[48,128,256]{2,1,0:T(8,128)(2,1)} %bitcast.4, s32[1024]{0:T(1024)S(1)} %pad_clamp_fusion), kind=kCustom, calls=%fused_computation.1 | custom fusion | bytes 3145824 | tf_op jit(solution)/shard_map/gather | solution.py:74
  108.6 3.1 %copy.53 = bf16[96,8,8,128]{3,2,1,0:T(8,128)(2,1)} copy(bf16[96,8,8,128]{3,1,2,0:T(8,128)(2,1)} %bitcast.64) | data formatting | bytes 3145728
  112.2 41.4 %all-gather.3.cloned.1.call-done = bf16[24,128,1024]{2,1,0:T(8,128)(2,1)} async-done(((bf16[24,128,256]{2,1,0:T(8,128)(2,1)}), bf16[24,128,1024]{2,1,0:T(8,128)(2,1)}) %all-gather.3.cloned.1.call-update) | async-done | bytes 6291472 | tf_op jit(solution)/shard_map/all_gather | solution.py:76
  153.6 9.8 %convolution_convert_fusion = bf16[3072,1024]{1,0:T(8,128)(2,1)S(1)} fusion(bf16[3072,1024]{1,0:T(8,128)(2,1)} %bitcast.70, bf16[1024,1024]{1,0:T(8,128)(2,1)S(1)} %copy-done), kind=kOutput, calls=%fused_computation.19 | convolution fusion | flops 6445596672 | bytes 14680064 | tf_op jit(solution)/shard_map/dot_general | solution.py:78
  163.5 7.2 %convolution_convert_fusion.1 = bf16[3072,1024]{1,0:T(8,128)(2,1)S(1)} fusion(bf16[3072,1024]{1,0:T(8,128)(2,1)S(1)} %bitcast.71, bf16[1024,1024]{1,0:T(8,128)(2,1)S(1)} %copy-done.6), kind=kOutput, calls=%fused_computation.20 | convolution fusion | flops 6445596672 | bytes 14680064 | tf_op jit(solution)/shard_map/dot_general | solution.py:79
  172.8 3.4 %collective-permute-start.2 = (bf16[256,1024]{1,0:T(8,128)(2,1)}, bf16[256,1024]{1,0:T(8,128)(2,1)S(1)}, u32[]{:S(2)}, u32[]{:S(2)}) collective-permute-start(bf16[256,1024]{1,0:T(8,128)(2,1)} %slice.32), channel_id=1, source_target_pairs={{0,4},{4,8},{8,12},{1,5},{5,9},{9,13},{2,6},{6,10},{10,14},{3,7},{... | collective-permute-start | bytes 1572872 | tf_op jit(solution)/shard_map/ppermute | solution.py:21
  176.3 4.2 %collective-permute-start.1 = (bf16[256,1024]{1,0:T(8,128)(2,1)}, bf16[256,1024]{1,0:T(8,128)(2,1)}, u32[]{:S(2)}, u32[]{:S(2)}) collective-permute-start(bf16[256,1024]{1,0:T(8,128)(2,1)} %slice.34), channel_id=1, source_target_pairs={{0,4},{4,8},{8,12},{1,5},{5,9},{9,13},{2,6},{6,10},{10,14},{3,7},{... | collective-permute-start | bytes 1572872 | tf_op jit(solution)/shard_map/ppermute | solution.py:21
  180.4 4.0 %slice_bitcast_fusion = bf16[352,8,8,128]{3,1,2,0:T(8,128)(2,1)S(1)} fusion(bf16[3072,1024]{1,0:T(8,128)(2,1)} %copy-done.2), kind=kLoop, calls=%fused_computation.17 | loop fusion | bytes 11534336
  184.4 1.5 copy.55
  185.9 4.2 %copy.44 = bf16[11,256,8,128]{3,1,2,0:T(8,128)(2,1)} copy(bf16[11,256,8,128]{3,2,1,0:T(8,128)(2,1)S(1)} %bitcast.57) | data formatting | bytes 11534336 | tf_op jit(solution)/shard_map/concatenate | solution.py:89
  191.5 1.5 copy.52
  193.0 1.6 copy.47
  194.8 4.6 %collective-permute-done.1 = bf16[256,1024]{1,0:T(8,128)(2,1)} collective-permute-done((bf16[256,1024]{1,0:T(8,128)(2,1)}, bf16[256,1024]{1,0:T(8,128)(2,1)}, u32[]{:S(2)}, u32[]{:S(2)}) %collective-permute-start.1) | collective-permute-done | bytes 524320 | tf_op jit(solution)/shard_map/ppermute | solution.py:21
  200.6 2.7 %fusion.1 = f32[12,8,256,64]{2,3,1,0:T(8,128)S(1)} fusion(bf16[11,256,8,128]{3,1,2,0:T(8,128)(2,1)S(1)} %copy.47, bf16[1,256,8,128]{3,1,2,0:T(8,128)(2,1)S(1)} %copy.46, bf16[12,64,8,128]{3,2,1,0:T(8,128)(2,1)S(1)} %bitcast.60), kind=kOutput, calls=%fused_computation.3 | convolution fusion | flops 405798912 | bytes 14155776 | tf_op jit(solution)/shard_map/gqhd,gkhd->ghqk/dot_general | solution.py:32
  203.3 4.3 %fusion.31 = (f32[12,8,64]{2,1,0:T(8,128)S(1)}, f32[12,8,64,256]{3,2,1,0:T(8,128)}) fusion(f32[12,8,256,64]{2,3,1,0:T(8,128)S(1)} %fusion.1, pred[12,256]{1,0:T(8,128)(4,1)S(1)} %bitcast.68), kind=kOutput, calls=%fused_computation.56 | output fusion | flops 9437439 | bytes 12610560 | tf_op jit(solution)/shard_map/sub | solution.py:40
  207.5 6.0 %fusion.20 = bf16[12,64,8,128]{3,1,2,0:T(8,128)(2,1)S(1)} fusion(pred[12]{0:T(512)(128)(4,1)S(1)} %get-tuple-element.5, bf16[11,256,8,128]{3,1,2,0:T(8,128)(2,1)} %copy.44, bf16[1,256,8,128]{3,1,2,0:T(8,128)(2,1)S(1)} %copy.43, f32[12,8,64,256]{3,2,1,0:T(8,128)} %get-tuple-element.8, f32[12,8,64]{2,1,0:T(8,128)S(1)} %get-tuple-element.7), kind=kOutput, calls=%fused_computation.31 | convolution fusion | flops 419954688 | bytes 14180364 | tf_op jit(solution)/shard_map/ghqk,gkhd->gqhd/dot_general | solution.py:42
  214.8 1.6 copy.60
  (55 shorter events, 11.2 us)
Async XLA Ops:
  6.5 147.1 %copy-start = (bf16[1024,1024]{1,0:T(8,128)(2,1)S(1)}, bf16[1024,1024]{1,0:T(8,128)(2,1)}, u32[]{:S(2)}) copy-start(bf16[1024,1024]{1,0:T(8,128)(2,1)} %param.9) | copy-start | bytes 6291460
  9.3 16.0 %all-to-all-start = ((s32[4,1,12]{2,1,0:T(1,128)}), s32[4,1,12]{2,1,0:T(1,128)S(1)}, u32[]{:S(2)}, u32[]{:S(2)}) async-start(s32[4,1,12]{2,1,0:T(1,128)} %bitcast.1), calls=%async_computation | async-start | bytes 4096 | tf_op jit(solution)/shard_map/all_to_all | solution.py:68
  25.4 7.4 %copy-start.4 = (s32[12,2]{0,1:T(2,128)S(1)}, s32[12,2]{0,1:T(2,128)}, u32[]{:S(2)}) copy-start(s32[12,2]{0,1:T(2,128)} %param.13) | copy-start | bytes 292
  28.0 79.1 %copy-start.7 = (s32[12]{0:T(128)S(1)}, s32[12]{0:T(128)}, u32[]{:S(2)}) copy-start(s32[12]{0:T(128)} %param.15) | copy-start | bytes 148
  28.0 75.4 %all-to-all-start.1 = ((bf16[4,12,128,256]{3,2,1,0:T(8,128)(2,1)}), bf16[4,12,128,256]{3,2,1,0:T(8,128)(2,1)}, u32[]{:S(2)}, u32[]{:S(2)}) async-start(bf16[4,12,128,256]{3,2,1,0:T(8,128)(2,1)} %bitcast.59), calls=%async_computation.1 | async-start | bytes 6291456 | tf_op jit(solution)/shard_map/all_to_all | solution.py:67
  32.9 120.7 %all-gather.3.cloned.1.call-start = ((), (), s32[]{:S(2)}) async-start(), calls=%async_computation.2 | async-start | bytes 7864320 | tf_op jit(solution)/shard_map/all_gather | solution.py:76
  107.3 4.4 %collective-permute-start = (bf16[2]{0:T(256)(128)(2,1)S(1)}, bf16[2]{0:T(256)(128)(2,1)S(1)}, u32[]{:S(2)}, u32[]{:S(2)}) collective-permute-start(bf16[2]{0:T(256)(128)(2,1)S(1)} %slice_reduce_fusion), channel_id=1, source_target_pairs={{0,4},{4,8},{8,12},{1,5},{5,9},{9,13},{2,6},{6,10},{10,14},{3,7},{... | collective-permute-start | bytes 20 | tf_op jit(solution)/shard_map/ppermute | solution.py:21
  153.6 9.9 %copy-start.5 = (bf16[24,128,1024]{2,1,0:T(8,128)(2,1)S(1)}, bf16[24,128,1024]{2,1,0:T(8,128)(2,1)}, u32[]{:S(2)}) copy-start(bf16[24,128,1024]{2,1,0:T(8,128)(2,1)} %all-gather.3.cloned.1.call-done) | copy-start | bytes 18874372
  153.6 9.9 %copy-start.6 = (bf16[1024,1024]{1,0:T(8,128)(2,1)S(1)}, bf16[1024,1024]{1,0:T(8,128)(2,1)}, u32[]{:S(2)}) copy-start(bf16[1024,1024]{1,0:T(8,128)(2,1)} %param.10) | copy-start | bytes 6291460
  170.7 5.6 %copy-start.2 = (bf16[3072,1024]{1,0:T(8,128)(2,1)}, bf16[3072,1024]{1,0:T(8,128)(2,1)S(1)}, u32[]{:S(2)}) copy-start(bf16[3072,1024]{1,0:T(8,128)(2,1)S(1)} %convolution_convert_fusion.1) | copy-start | bytes 18874372
  172.8 21.8 %collective-permute-start.2 = (bf16[256,1024]{1,0:T(8,128)(2,1)}, bf16[256,1024]{1,0:T(8,128)(2,1)S(1)}, u32[]{:S(2)}, u32[]{:S(2)}) collective-permute-start(bf16[256,1024]{1,0:T(8,128)(2,1)} %slice.32), channel_id=1, source_target_pairs={{0,4},{4,8},{8,12},{1,5},{5,9},{9,13},{2,6},{6,10},{10,14},{3,7},{... | collective-permute-start | bytes 1572872 | tf_op jit(solution)/shard_map/ppermute | solution.py:21
  176.3 23.1 %collective-permute-start.1 = (bf16[256,1024]{1,0:T(8,128)(2,1)}, bf16[256,1024]{1,0:T(8,128)(2,1)}, u32[]{:S(2)}, u32[]{:S(2)}) collective-permute-start(bf16[256,1024]{1,0:T(8,128)(2,1)} %slice.34), channel_id=1, source_target_pairs={{0,4},{4,8},{8,12},{1,5},{5,9},{9,13},{2,6},{6,10},{10,14},{3,7},{... | collective-permute-start | bytes 1572872 | tf_op jit(solution)/shard_map/ppermute | solution.py:21
  193.0 7.6 %copy-start.3 = (bf16[96,8,8,128]{3,2,1,0:T(8,128)(2,1)S(1)}, bf16[96,8,8,128]{3,2,1,0:T(8,128)(2,1)}, u32[]{:S(2)}) copy-start(bf16[96,8,8,128]{3,2,1,0:T(8,128)(2,1)} %copy.53) | copy-start | bytes 4718596
  207.5 8.9 %copy-start.1 = (bf16[1024,1024]{1,0:T(8,128)(2,1)S(1)}, bf16[1024,1024]{1,0:T(8,128)(2,1)}, u32[]{:S(2)}) copy-start(bf16[1024,1024]{1,0:T(8,128)(2,1)} %param.9) | copy-start | bytes 6291460
Sparse Core Ops, SparseCore 0:
  107.3 46.3 all-gather.2
where the time goes:
time: 224 us; the launch traced here: 223 us
  waiting for transfers between devices  116 us (52%)
  local copies, waits for them, and re-layouts  33.2 us (15%)
  matrix products  25.7 us (11%)
  starting transfers between devices  20 us (9%)
  between operations  13.7 us (6%)
  other arithmetic  7.84 us (4%)
  blocking collectives  6.48 us (3%)
    all_to_all x1, waiting for transfers between devices, body(): lax.all_to_all(normed[lax.all_to_all(table, 'seq', split_axis=0, concat_a...  70.3 us
    all_gather x1, waiting for transfers between devices, body(): piece = lax.all_gather(fetched, ('mp', 'rep'), axis=2, tiled=True)  41.4 us
    unnamed x28, local copies, waits for them, and re-layouts  16 us
    dot_general x1, matrix products, body(): keys = jnp.dot(flat, key_weight, preferred_element_type=jnp.float32)  9.85 us
    ppermute x3, starting transfers between devices, from_behind(): lax.ppermute(value, axis, [(source, source + steps) for source in range(f...  8.84 us
    dot_general x1, matrix products, body(): values = jnp.dot(flat, value_weight, preferred_element_type=jnp.float32)  7.16 us
    psum x1, blocking collectives, body(): squares = lax.psum(jnp.sum(raw * raw, axis=2), ('mp', 'rep'))  6.48 us
    all_to_all x1, starting transfers between devices, body(): lax.all_to_all(table, 'seq', split_axis=0, concat_axis=0, tiled=True)  6.32 us
  transfers between devices with their start and end apart: 6, of which 3 were waited for; matrix products, arithmetic and copies ran while one was open for 10% of the time, Pallas kernels for 0%

commit v1 on v0

v1 whole, which is shorter than its diff:
```python
import math

import jax
import jax.numpy as jnp
from jax import lax
from jax.experimental import pallas as pl
from jax.experimental.pallas import tpu as pltpu
from jax.sharding import PartitionSpec as P

HEAD_DIM = 128
DE = 1024
NLEN = 128
STRETCH = 64
KMAX = 2
EPS = 1e-06

SEQ_SPEC = ("parts", "seq")
FEATURES = ("mp", "rep")
VMEM_LIMIT = 48 * 1024 * 1024


def shifted(value, axis, steps):
    count = lax.axis_size(axis)
    first, last = max(0, -steps), min(count, count - steps)
    return lax.ppermute(value, axis, [(source, source + steps) for source in range(first, last)])


def swapped(value, axis):
    return lax.ppermute(value, axis, [(0, 1), (1, 0)])


def project_kernel(places, gain_ref, *refs):
    *pieces, key_weight, value_weight, keys_out, values_out, normed = refs
    rows = normed.shape[0]
    width = pieces[0].shape[2]
    raw = [piece[...].reshape(rows, width).astype(jnp.float32) for piece in pieces]
    squares = sum(jnp.sum(part * part, axis=1, keepdims=True) for part in raw)
    scale = lax.rsqrt(squares / DE + EPS)
    for index, part in enumerate(raw):
        start = pl.multiple_of(places[index] * width, width)
        normed[:, pl.ds(start, width)] = (part * scale * gain_ref[:, pl.ds(start, width)]).astype(jnp.bfloat16)
    states = normed[...]
    for weight, out in ((key_weight, keys_out), (value_weight, values_out)):
        out[...] = jnp.dot(states, weight[...], preferred_element_type=jnp.float32).astype(jnp.bfloat16).reshape(out.shape)


def project(places, gain, pieces, key_weight, value_weight, group):
    count, tokens, width = pieces[0].shape
    columns = key_weight.shape[1]
    out = jax.ShapeDtypeStruct((count, tokens, columns), jnp.bfloat16)
    piece_spec = pl.BlockSpec((group, tokens, width), lambda i, _: (i, 0, 0))
    weight_spec = pl.BlockSpec((DE, columns), lambda i, _: (0, 0))
    out_spec = pl.BlockSpec((group, tokens, columns), lambda i, _: (i, 0, 0))
    return pl.pallas_call(
        project_kernel,
        out_shape=(out, out),
        grid_spec=pltpu.PrefetchScalarGridSpec(
            num_scalar_prefetch=1,
            grid=(count // group,),
            in_specs=[pl.BlockSpec((1, DE), lambda i, _: (0, 0))] + [piece_spec] * len(pieces) + [weight_spec] * 2,
            out_specs=(out_spec, out_spec),
            scratch_shapes=[pltpu.VMEM((group * tokens, DE), jnp.bfloat16)],
        ),
        compiler_params=pltpu.CompilerParams(vmem_limit_bytes=VMEM_LIMIT),
        cost_estimate=pl.CostEstimate(
            flops=4 * count * tokens * DE * columns,
            bytes_accessed=2 * (count * tokens * (DE + 2 * columns) + 2 * DE * columns),
            transcendentals=0,
        ),
        name="project",
    )(places, gain, *pieces, key_weight, value_weight)


def attend_kernel(slots, counts, query_ref, first_keys, second_keys, first_values, second_values, out_ref):
    stretch = pl.program_id(0)
    count = counts[stretch]

    @pl.when(count == 0)
    def _():
        out_ref[...] = jnp.zeros_like(out_ref)

    @pl.when(count > 0)
    def _():
        columns = query_ref.shape[1]
        span = lax.broadcasted_iota(jnp.int32, (1, KMAX * NLEN), 1)
        allowed = span < count * NLEN
        for head in range(columns // HEAD_DIM):
            part = slice(head * HEAD_DIM, (head + 1) * HEAD_DIM)
            keys = jnp.concatenate([first_keys[0, :, part], second_keys[0, :, part]], axis=0)
            values = jnp.concatenate([first_values[0, :, part], second_values[0, :, part]], axis=0)
            scores = lax.dot_general(
                query_ref[:, part], keys, (((1,), (1,)), ((), ())), preferred_element_type=jnp.float32
            ) * (1.0 / math.sqrt(HEAD_DIM))
            scores = jnp.where(allowed, scores, -1e30)
            expo = jnp.exp(scores - jnp.max(scores, axis=1, keepdims=True))
            weights = (expo / jnp.sum(expo, axis=1, keepdims=True)).astype(jnp.bfloat16)
            out_ref[:, part] = jnp.dot(weights, values, preferred_element_type=jnp.float32).astype(jnp.bfloat16)


def attend(slots, counts, queries, keys, values):
    stretches = counts.shape[0]
    columns = queries.shape[1]

    def entry(k):
        return pl.BlockSpec((1, NLEN, columns), lambda i, slots, _: (slots[i * KMAX + k], 0, 0))

    query_spec = pl.BlockSpec((STRETCH, columns), lambda i, *_: (i, 0))
    return pl.pallas_call(
        attend_kernel,
        out_shape=jax.ShapeDtypeStruct(queries.shape, jnp.bfloat16),
        grid_spec=pltpu.PrefetchScalarGridSpec(
            num_scalar_prefetch=2,
            grid=(stretches,),
            in_specs=[query_spec, entry(0), entry(1), entry(0), entry(1)],
            out_specs=query_spec,
        ),
        compiler_params=pltpu.CompilerParams(vmem_limit_bytes=VMEM_LIMIT),
        cost_estimate=pl.CostEstimate(
            flops=4 * stretches * STRETCH * KMAX * NLEN * columns,
            bytes_accessed=4 * stretches * columns * (STRETCH + KMAX * NLEN),
            transcendentals=stretches * STRETCH * KMAX * NLEN * columns // HEAD_DIM,
        ),
        name="attend",
    )(slots, counts, queries, keys, keys, values, values)


def previous_rows(nbr_owner, nbr_slot, nbr_count):
    rows = jnp.concatenate([nbr_owner, nbr_slot, nbr_count[:, None]], axis=1)
    rows = jnp.concatenate([shifted(rows[-1:], "seq", 1), rows[:-1]], axis=0)
    return rows[:, :KMAX], rows[:, KMAX : 2 * KMAX], rows[:, 2 * KMAX]


def fetch_by_request(store, owners, slots):
    owners_axis = lax.axis_size("seq")
    stretches = owners.shape[0]
    depth = min(stretches, max(2, 2 * stretches * KMAX // owners_axis) + 1)
    owners, slots = owners.reshape(-1), slots.reshape(-1)
    order = jnp.arange(owners.shape[0], dtype=jnp.int32)
    before = (owners[:, None] == owners[None, :]) & (order[None, :] < order[:, None])
    target = owners * depth + jnp.sum(before.astype(jnp.int32), axis=1)
    hits = target[:, None] == jnp.arange(owners_axis * depth, dtype=jnp.int32)[None, :]
    table = jnp.sum(jnp.where(hits, slots[:, None], 0), axis=0).reshape(owners_axis, depth)
    asked = lax.all_to_all(table, "seq", split_axis=0, concat_axis=0, tiled=True)
    arrived = lax.all_to_all(store[asked], "seq", split_axis=0, concat_axis=0, tiled=True)
    fetched = arrived.reshape(owners_axis * depth, NLEN, store.shape[2])[target]
    return [lax.all_gather(fetched, FEATURES, axis=2, tiled=True)], jnp.zeros((1,), jnp.int32)


def fetch_all(store, owners, slots):
    seq = lax.axis_index("seq")
    size = lax.axis_size("seq")
    everything = [store]
    for distance in range(1, size):
        for steps in (distance, -distance):
            everything.append(shifted(store, "seq", steps))
    ahead = owners - seq
    place = jnp.where(ahead == 0, 0, jnp.where(ahead < 0, -2 * ahead - 1, 2 * ahead))
    pool = jnp.concatenate(everything, axis=0)
    mine = pool[(place * store.shape[0] + slots).reshape(-1)]
    across = swapped(mine, "mp")
    pieces = [mine, swapped(mine, "rep"), across, swapped(across, "rep")]
    block = 2 * lax.axis_index("mp") + lax.axis_index("rep")
    return pieces, jnp.stack([block, block ^ 1, block ^ 2, block ^ 3]).astype(jnp.int32)


def body(queries, key_weight, value_weight, enc_gain, store, nbr_owner, nbr_slot, nbr_count):
    stretches = nbr_owner.shape[0]
    gain = lax.all_gather(enc_gain, FEATURES, axis=0, tiled=True)[None]
    owners, slots, counts = previous_rows(nbr_owner, nbr_slot, nbr_count)
    small = lax.axis_size("seq") <= 4 and lax.axis_size("mp") == 2 and lax.axis_size("rep") == 2
    pieces, places = (fetch_all if small else fetch_by_request)(store, owners, slots)
    keys, values = project(places, gain, pieces, key_weight, value_weight, 4)
    order = jnp.arange(stretches * KMAX, dtype=jnp.int32)
    return attend(order, counts, queries, keys, values)


def solution(mesh):
    in_specs = (
        P(SEQ_SPEC, FEATURES),
        P(None, FEATURES),
        P(None, FEATURES),
        P(FEATURES),
        P(SEQ_SPEC, None, FEATURES),
        P(SEQ_SPEC, None),
        P(SEQ_SPEC, None),
        P(SEQ_SPEC),
    )
    out_specs = P(SEQ_SPEC, FEATURES)
    return jax.shard_map(body, mesh=mesh, in_specs=in_specs, out_specs=out_specs, check_vma=False)
```

time: 224 us -> 211 us (0.942)
  the two profiles are of different devices: /device:TPU:0 before, /device:TPU:19 now
where the time goes in v1:
time: 211 us; the launch traced here: 210 us
  waiting for transfers between devices  107 us (51%)
  Pallas kernels  57.5 us (27%)
  starting transfers between devices  23.4 us (11%)
  local copies, waits for them, and re-layouts  16.4 us (8%)
  blocking collectives  4.87 us (2%)
    ppermute x7, waiting for transfers between devices, shifted(): lax.ppermute(value, axis, [(source, source + steps) for source in range(f...  75.4 us
    pallas_call x1, Pallas kernels, attend(): pl.pallas_call(attend_kernel, out_shape=jax.ShapeDtypeStruct(queries.shap...  35.6 us
    ppermute x3, waiting for transfers between devices, swapped(): return lax.ppermute(value, axis, [(0, 1), (1, 0)])  31.7 us
    pallas_call x1, Pallas kernels, project(): pl.pallas_call(project_kernel, out_shape=(out, out), grid_spec=pltpu.Pref...  22 us
    ppermute x7, starting transfers between devices, shifted(): lax.ppermute(value, axis, [(source, source + steps) for source in range(f...  18.2 us
    unnamed x10, local copies, waits for them, and re-layouts  10.1 us
    ppermute x3, starting transfers between devices, swapped(): return lax.ppermute(value, axis, [(0, 1), (1, 0)])  5.21 us
    all_gather x1, blocking collectives, body(): gain = lax.all_gather(enc_gain, FEATURES, axis=0, tiled=True)[None]  4.87 us
  transfers between devices with their start and end apart: 10, of which 2 were waited for; matrix products, arithmetic and copies ran while one was open for 5% of the time, Pallas kernels for 0%

profile of v1, /device:TPU:19, one launch (start us, length us, event | category | flops | bytes accessed | tf_op | source)
XLA Modules:
  0.0 210.3 jit_solution(9397712903398706880)
XLA Ops:
  0.0 3.2 %collective-permute-start.1 = (bf16[16,128,256]{2,1,0:T(8,128)(2,1)}, bf16[16,128,256]{2,1,0:T(8,128)(2,1)}, u32[]{:S(2)}, u32[]{:S(2)}) collective-permute-start(bf16[16,128,256]{2,1,0:T(8,128)(2,1)} %param.12), channel_id=1, source_target_pairs={{0,4},{4,8},{8,12},{1,5},{5,9},{9,13},{2,6},{6,10},{10,14},{3,7},{... | collective-permute-start | bytes 3145736 | tf_op jit(solution)/shard_map/ppermute | solution.py:25
  3.2 2.1 collective-permute-start.2
  5.3 1.3 collective-permute-start.3
  6.6 5.0 %collective-permute-start.4 = (bf16[16,128,256]{2,1,0:T(8,128)(2,1)}, bf16[16,128,256]{2,1,0:T(8,128)(2,1)S(1)}, u32[]{:S(2)}, u32[]{:S(2)}) collective-permute-start(bf16[16,128,256]{2,1,0:T(8,128)(2,1)} %param.12), channel_id=1, source_target_pairs={{8,0},{12,4},{9,1},{13,5},{10,2},{14,6},{11,3},{15,7},{24,16},{28,... | collective-permute-start | bytes 3145736 | tf_op jit(solution)/shard_map/ppermute | solution.py:25
  11.6 0.7 pad_add_fusion
  12.4 3.3 %collective-permute-start = (s32[1,5]{0,1:T(8,128)S(1)}, s32[1,5]{0,1:T(8,128)S(1)}, u32[]{:S(2)}, u32[]{:S(2)}) collective-permute-start(s32[1,5]{0,1:T(8,128)S(1)} %slice.15), channel_id=1, source_target_pairs={{0,4},{4,8},{8,12},{1,5},{5,9},{9,13},{2,6},{6,10},{10,14},{3,7},{... | collective-permute-start | bytes 68 | tf_op jit(solution)/shard_map/ppermute | solution.py:25
  15.7 2.3 %constant_dynamic-update-slice_fusion.6 = bf16[112,128,256]{2,1,0:T(8,128)(2,1)} fusion(bf16[16,128,256]{2,1,0:T(8,128)(2,1)} %param.12), kind=kLoop, calls=%fused_computation.7 | loop fusion | bytes 2097152
  18.0 75.4 %collective-permute-done = s32[1,5]{0,1:T(8,128)S(1)} collective-permute-done((s32[1,5]{0,1:T(8,128)S(1)}, s32[1,5]{0,1:T(8,128)S(1)}, u32[]{:S(2)}, u32[]{:S(2)}) %collective-permute-start) | collective-permute-done | bytes 52 | tf_op jit(solution)/shard_map/ppermute | solution.py:25
  93.3 1.7 collective-permute-start.5
  95.1 1.7 collective-permute-start.6
  97.0 2.3 %constant_dynamic-update-slice_fusion.5 = bf16[112,128,256]{2,1,0:T(8,128)(2,1)} fusion(bf16[112,128,256]{2,1,0:T(8,128)(2,1)} %constant_dynamic-update-slice_fusion.6, bf16[16,128,256]{2,1,0:T(8,128)(2,1)} %collective-permute-done.1), kind=kLoop, calls=%fused_computation.6 | loop fusion | bytes 2097152
  99.3 1.0 constant_dynamic-update-slice_fusion.4
  100.4 1.1 constant_dynamic-update-slice_fusion.3
  101.5 1.0 constant_dynamic-update-slice_fusion.2
  102.5 2.3 %constant_dynamic-update-slice_fusion.1 = bf16[112,128,256]{2,1,0:T(8,128)(2,1)} fusion(bf16[112,128,256]{2,1,0:T(8,128)(2,1)} %constant_dynamic-update-slice_fusion.2, bf16[16,128,256]{2,1,0:T(8,128)(2,1)} %collective-permute-done.5), kind=kLoop, calls=%fused_computation.2 | loop fusion | bytes 2097152
  104.8 2.3 %constant_dynamic-update-slice_fusion = bf16[112,128,256]{2,1,0:T(8,128)(2,1)} fusion(bf16[112,128,256]{2,1,0:T(8,128)(2,1)} %constant_dynamic-update-slice_fusion.1, bf16[16,128,256]{2,1,0:T(8,128)(2,1)} %collective-permute-done.6), kind=kLoop, calls=%fused_computation.1 | loop fusion | bytes 2097152 | tf_op jit(solution)/shard_map/concatenate | solution.py:158
  107.1 3.7 %gather_fusion = bf16[24,128,256]{2,1,0:T(8,128)(2,1)S(1)} fusion(bf16[112,128,256]{2,1,0:T(8,128)(2,1)} %constant_dynamic-update-slice_fusion, s32[1024]{0:T(1024)S(1)} %pad_clamp_fusion), kind=kCustom, calls=%fused_computation | custom fusion | bytes 3145824 | tf_op jit(solution)/shard_map/gather | solution.py:159
  110.9 0.3 collective-permute-start.8
  111.2 2.1 %collective-permute-start.7 = (bf16[24,128,256]{2,1,0:T(8,128)(2,1)S(1)}, bf16[24,128,256]{2,1,0:T(8,128)(2,1)}, u32[]{:S(2)}, u32[]{:S(2)}) collective-permute-start(bf16[24,128,256]{2,1,0:T(8,128)(2,1)S(1)} %gather_fusion), channel_id=1, source_target_pairs={{0,1},{1,0},{2,3},{3,2},{4,5},{5,4},{6,7},{7,6},{8,9},{9,8},{10,11... | collective-permute-start | bytes 4718600 | tf_op jit(solution)/shard_map/ppermute | solution.py:29
  113.3 31.7 %collective-permute-done.8.refs_2_ = bf16[24,128,256]{2,1,0:T(8,128)(2,1)S(1)} collective-permute-done((bf16[24,128,256]{2,1,0:T(8,128)(2,1)S(1)}, bf16[24,128,256]{2,1,0:T(8,128)(2,1)S(1)}, u32[]{:S(2)}, u32[]{:S(2)}) %collective-permute-start.8) | collective-permute-done | bytes 1572896 | tf_op jit(solution)/shard_map/ppermute | solution.py:29
  145.0 2.8 %collective-permute-start.9 = (bf16[24,128,256]{2,1,0:T(8,128)(2,1)S(1)}, bf16[24,128,256]{2,1,0:T(8,128)(2,1)}, u32[]{:S(2)}, u32[]{:S(2)}) collective-permute-start(bf16[24,128,256]{2,1,0:T(8,128)(2,1)S(1)} %collective-permute-done.8.refs_2_), channel_id=1, source_target_pairs={{0,1},{1,0},{2,3},{3,2},{4,5},{5,4},{6,7},{7,6},{8,9},{9,8},{10,11... | collective-permute-start | bytes 4718600 | tf_op jit(solution)/shard_map/ppermute | solution.py:29
  147.7 4.9 %all-gather = f32[4,1,256]{2,1,0:T(1,128)S(1)} all-gather(f32[1,1,256]{2,1,0:T(1,128)S(1)} %bitcast.14), channel_id=1, replica_groups=mesh['parts'=2,'seq'=4,'mp'=2,'rep'=2] {'mp','rep'}, dimensions={0}, use_global_device_ids=true | all-gather | bytes 5120 | tf_op jit(solution)/shard_map/all_gather | solution.py:168
  152.7 22.0 %project.1 = (bf16[24,128,1024]{2,1,0:T(8,128)(2,1)}, bf16[24,128,1024]{2,1,0:T(8,128)(2,1)}) custom-call(s32[4]{0:T(128)S(1)} %pad_add_fusion.2.places, f32[1,1024]{1,0:T(1,128)S(1)} %bitcast.12, bf16[24,128,256]{2,1,0:T(8,128)(2,1)S(1)} %gather_fusion, bf16[24,128,256]{2,1,0:T(8,128)(2,1)} %collective-permute-done.7.refs_1_, ...), custom_call_target="tpu_custom_call" | custom-call | flops 12884901888 | bytes 23068672 | tf_op jit(solution)/shard_map/project/pallas_call | solution.py:54
  174.7 35.6 %attend.1 = bf16[768,1024]{1,0:T(8,128)(2,1)} custom-call(s32[24]{0:T(128)S(1)} %iota.3.slots, s32[12]{0:T(128)S(1)} %slice_bitcast_fusion.counts, bf16[768,1024]{1,0:T(8,128)(2,1)S(1)} %copy-done, bf16[24,128,1024]{2,1,0:T(8,128)(2,1)} %get-tuple-element.7.first_keys.second_keys, bf16[24,128,1024]{2,1,0:T(8,128)(2,1)} %get-tuple-element.7.first_keys.second_keys, ...), custom_call_target="tpu_custom_call" | custom-call | flops 805306368 | bytes 15728640 | tf_op jit(solution)/shard_map/attend/pallas_call | solution.py:108
  (22 shorter events, 0.5 us)
Async XLA Ops:
  0.0 95.1 %collective-permute-start.1 = (bf16[16,128,256]{2,1,0:T(8,128)(2,1)}, bf16[16,128,256]{2,1,0:T(8,128)(2,1)}, u32[]{:S(2)}, u32[]{:S(2)}) collective-permute-start(bf16[16,128,256]{2,1,0:T(8,128)(2,1)} %param.12), channel_id=1, source_target_pairs={{0,4},{4,8},{8,12},{1,5},{5,9},{9,13},{2,6},{6,10},{10,14},{3,7},{... | collective-permute-start | bytes 3145736 | tf_op jit(solution)/shard_map/ppermute | solution.py:25
  3.2 96.1 %collective-permute-start.2 = (bf16[16,128,256]{2,1,0:T(8,128)(2,1)}, bf16[16,128,256]{2,1,0:T(8,128)(2,1)S(1)}, u32[]{:S(2)}, u32[]{:S(2)}) collective-permute-start(bf16[16,128,256]{2,1,0:T(8,128)(2,1)} %param.12), channel_id=1, source_target_pairs={{4,0},{8,4},{12,8},{5,1},{9,5},{13,9},{6,2},{10,6},{14,10},{7,3},{... | collective-permute-start | bytes 3145736 | tf_op jit(solution)/shard_map/ppermute | solution.py:25
  5.3 95.1 %collective-permute-start.3 = (bf16[16,128,256]{2,1,0:T(8,128)(2,1)}, bf16[16,128,256]{2,1,0:T(8,128)(2,1)S(1)}, u32[]{:S(2)}, u32[]{:S(2)}) collective-permute-start(bf16[16,128,256]{2,1,0:T(8,128)(2,1)} %param.12), channel_id=1, source_target_pairs={{0,8},{4,12},{1,9},{5,13},{2,10},{6,14},{3,11},{7,15},{16,24},{20,... | collective-permute-start | bytes 3145736 | tf_op jit(solution)/shard_map/ppermute | solution.py:25
  6.6 94.9 %collective-permute-start.4 = (bf16[16,128,256]{2,1,0:T(8,128)(2,1)}, bf16[16,128,256]{2,1,0:T(8,128)(2,1)S(1)}, u32[]{:S(2)}, u32[]{:S(2)}) collective-permute-start(bf16[16,128,256]{2,1,0:T(8,128)(2,1)} %param.12), channel_id=1, source_target_pairs={{8,0},{12,4},{9,1},{13,5},{10,2},{14,6},{11,3},{15,7},{24,16},{28,... | collective-permute-start | bytes 3145736 | tf_op jit(solution)/shard_map/ppermute | solution.py:25
  12.4 80.9 %collective-permute-start = (s32[1,5]{0,1:T(8,128)S(1)}, s32[1,5]{0,1:T(8,128)S(1)}, u32[]{:S(2)}, u32[]{:S(2)}) collective-permute-start(s32[1,5]{0,1:T(8,128)S(1)} %slice.15), channel_id=1, source_target_pairs={{0,4},{4,8},{8,12},{1,5},{5,9},{9,13},{2,6},{6,10},{10,14},{3,7},{... | collective-permute-start | bytes 68 | tf_op jit(solution)/shard_map/ppermute | solution.py:25
  93.3 9.2 %collective-permute-start.5 = (bf16[16,128,256]{2,1,0:T(8,128)(2,1)}, bf16[16,128,256]{2,1,0:T(8,128)(2,1)}, u32[]{:S(2)}, u32[]{:S(2)}) collective-permute-start(bf16[16,128,256]{2,1,0:T(8,128)(2,1)} %param.12), channel_id=1, source_target_pairs={{0,12},{1,13},{2,14},{3,15},{16,28},{17,29},{18,30},{19,31}} | collective-permute-start | bytes 3145736 | tf_op jit(solution)/shard_map/ppermute | solution.py:25
  95.1 9.7 %collective-permute-start.6 = (bf16[16,128,256]{2,1,0:T(8,128)(2,1)}, bf16[16,128,256]{2,1,0:T(8,128)(2,1)}, u32[]{:S(2)}, u32[]{:S(2)}) collective-permute-start(bf16[16,128,256]{2,1,0:T(8,128)(2,1)} %param.12), channel_id=1, source_target_pairs={{12,0},{13,1},{14,2},{15,3},{28,16},{29,17},{30,18},{31,19}} | collective-permute-start | bytes 3145736 | tf_op jit(solution)/shard_map/ppermute | solution.py:25
  99.3 48.4 %copy-start.1 = (f32[256]{0:T(256)S(1)}, f32[256]{0:T(256)}, u32[]{:S(2)}) copy-start(f32[256]{0:T(256)} %param.11) | copy-start | bytes 3076
  110.9 34.1 %collective-permute-start.8 = (bf16[24,128,256]{2,1,0:T(8,128)(2,1)S(1)}, bf16[24,128,256]{2,1,0:T(8,128)(2,1)S(1)}, u32[]{:S(2)}, u32[]{:S(2)}) collective-permute-start(bf16[24,128,256]{2,1,0:T(8,128)(2,1)S(1)} %gather_fusion), channel_id=1, source_target_pairs={{0,2},{2,0},{1,3},{3,1},{4,6},{6,4},{5,7},{7,5},{8,10},{10,8},{9,1... | collective-permute-start | bytes 4718600 | tf_op jit(solution)/shard_map/ppermute | solution.py:29
  111.2 41.5 %collective-permute-start.7 = (bf16[24,128,256]{2,1,0:T(8,128)(2,1)S(1)}, bf16[24,128,256]{2,1,0:T(8,128)(2,1)}, u32[]{:S(2)}, u32[]{:S(2)}) collective-permute-start(bf16[24,128,256]{2,1,0:T(8,128)(2,1)S(1)} %gather_fusion), channel_id=1, source_target_pairs={{0,1},{1,0},{2,3},{3,2},{4,5},{5,4},{6,7},{7,6},{8,9},{9,8},{10,11... | collective-permute-start | bytes 4718600 | tf_op jit(solution)/shard_map/ppermute | solution.py:29
  145.0 7.7 %collective-permute-start.9 = (bf16[24,128,256]{2,1,0:T(8,128)(2,1)S(1)}, bf16[24,128,256]{2,1,0:T(8,128)(2,1)}, u32[]{:S(2)}, u32[]{:S(2)}) collective-permute-start(bf16[24,128,256]{2,1,0:T(8,128)(2,1)S(1)} %collective-permute-done.8.refs_2_), channel_id=1, source_target_pairs={{0,1},{1,0},{2,3},{3,2},{4,5},{5,4},{6,7},{7,6},{8,9},{9,8},{10,11... | collective-permute-start | bytes 4718600 | tf_op jit(solution)/shard_map/ppermute | solution.py:29
  152.7 22.0 %copy-start = (bf16[768,1024]{1,0:T(8,128)(2,1)S(1)}, bf16[768,1024]{1,0:T(8,128)(2,1)}, u32[]{:S(2)}) copy-start(bf16[768,1024]{1,0:T(8,128)(2,1)} %query_ref.1) | copy-start | bytes 4718596
